TPU v7x, 32 devices: a whole 2x2x4 slice. The times are simulated.
32 devices in a mesh: row: 4 (over y, core), col: 8 (over z, x).
Axes of the slice: x: 2, y: 2, z: 4, core: 2. Of those that a mesh axis runs over, the one named last changes fastest.
Arguments:
- tensor_tiles: bfloat16 [128, 128, 128, 128], P(('row', 'col')), may hold values from -384 to 384
- tile_mode1: int32 [128], P(('row', 'col')), may hold values from 0 to 255, as said below
- tile_mode2: int32 [128], P(('row', 'col')), may hold values from 0 to 63
- tile_mode3: int32 [128], P(('row', 'col')), may hold values from 0 to 31
- factor_mode2: bfloat16 [48, 8192], P(None, 'col'), may hold values from -1 to 1
- factor_mode3: bfloat16 [48, 4096], P(None, 'row'), may hold values from -1 to 1
Outputs:
- factor_mode1: float32 [48, 32768], P(None, ('row', 'col'))
Inputs may be any that keep to these rules, and one draw needn't show every extreme that they name: `tile_mode1`: tiles at positions g*32 to (g+1)*32 - 1 have mode-1 blocks in g*64 to (g+1)*64 - 1; the 4 tiles at positions d*4 to (d+1)*4 - 1 have mode-1 blocks in distinct groups of 8 consecutive blocks (block // 8 all different).
All inputs are finite; a program needn't handle non-finite values.
Results may differ from a plain program's by a relative error of at most 0.0003.
Values may be sent and summed in bfloat16 or wider, within the bound.
A program may use at most 128 MiB of HBM per device.

v0:
```python
import jax
import jax.numpy as jnp
from jax import lax
from jax.sharding import PartitionSpec as P

IB_DEV = 8


ridge_term = 0.5


def body(tensor_tiles, tile_mode1, tile_mode2, tile_mode3, factor_mode2, factor_mode3):
    rank_count = factor_mode2.shape[0]
    tile_edge = tensor_tiles.shape[1]
    gram_two = lax.psum(
        jnp.dot(factor_mode2, factor_mode2.T, preferred_element_type=jnp.float32), "col"
    )
    gram_three = lax.psum(
        jnp.dot(factor_mode3, factor_mode3.T, preferred_element_type=jnp.float32), "row"
    )
    system = gram_two * gram_three + ridge_term * jnp.eye(rank_count, dtype=jnp.float32)
    full_two = lax.all_gather(factor_mode2, "col", axis=1, tiled=True)
    full_three = lax.all_gather(factor_mode3, "row", axis=1, tiled=True)
    mode2_rows = jnp.transpose(
        full_two.reshape(rank_count, -1, tile_edge)[:, tile_mode2], (1, 0, 2)
    )
    mode3_rows = jnp.transpose(
        full_three.reshape(rank_count, -1, tile_edge)[:, tile_mode3], (1, 0, 2)
    )
    contracted = jnp.einsum(
        "trc,tabc->trab", mode3_rows, tensor_tiles, preferred_element_type=jnp.float32
    )
    tile_rows = jnp.einsum(
        "trab,trb->tra", contracted, mode2_rows.astype(jnp.float32), precision=lax.Precision.HIGHEST
    )
    col_count = lax.axis_size("col")
    row_blocks = IB_DEV * col_count
    local_blocks = tile_mode1 - lax.axis_index("row") * row_blocks
    owner_slot = local_blocks // IB_DEV
    block_within = local_blocks % IB_DEV
    matches = owner_slot[:, None] == jnp.arange(col_count, dtype=jnp.int32)[None, :]
    destination = matches.astype(jnp.float32)
    outgoing = jnp.einsum("tra,td->dra", tile_rows, destination, precision=lax.Precision.HIGHEST)
    outgoing_ids = jnp.sum(jnp.where(matches, block_within[:, None] + 1, 0), axis=0) - 1
    incoming, incoming_ids = (
        lax.all_to_all(outgoing, "col", split_axis=0, concat_axis=0, tiled=True),
        lax.all_to_all(outgoing_ids, "col", split_axis=0, concat_axis=0, tiled=True),
    )
    placing = (incoming_ids[:, None] == jnp.arange(IB_DEV, dtype=jnp.int32)[None, :]).astype(
        jnp.float32
    )
    right_side = jnp.einsum("sra,sb->rba", incoming, placing, precision=lax.Precision.HIGHEST)
    right_side = right_side.reshape(rank_count, IB_DEV * tile_edge)
    cholesky_factor = jnp.linalg.cholesky(system)
    middle = lax.linalg.triangular_solve(cholesky_factor, right_side, left_side=True, lower=True)
    return lax.linalg.triangular_solve(
        cholesky_factor, middle, left_side=True, lower=True, transpose_a=True
    )


def solution(mesh):
    in_specs = (
        P(("row", "col"), None, None, None),
        P(("row", "col")),
        P(("row", "col")),
        P(("row", "col")),
        P(None, "col"),
        P(None, "row"),
    )
    out_specs = P(None, ("row", "col"))
    return jax.shard_map(body, mesh=mesh, in_specs=in_specs, out_specs=out_specs, check_vma=False)
```

profile of v0, /device:TPU:1, one launch (start us, length us, event | category | flops | bytes accessed | tf_op | source)
XLA Modules:
  0.0 146.4 jit_solution(14127841998260885391)
XLA Ops:
  0.0 0.7 fusion.24
  0.7 0.7 and_select_fusion.1
  1.3 0.1 select_reduce_fusion.1
  1.4 0.7 copy.19
  2.1 6.4 %all-to-all-start = ((s32[8,1,1]{2,1,0:T(1,128)}), s32[8,1,1]{2,1,0:T(1,128)S(1)}, u32[]{:S(2)}, u32[]{:S(2)}) async-start(s32[8,1,1]{2,1,0:T(1,128)} %copy.19), calls=%async_computation | async-start | bytes 8192 | tf_op jit(solution)/shard_map/all_to_all | solution.py:47
  8.5 1.1 fusion.26
  9.6 7.5 %all_gather.6 = bf16[48,4096]{1,0:T(8,128)(2,1)S(1)} all-gather(bf16[48,1024]{1,0:T(8,128)(2,1)} %param.11), channel_id=1, replica_groups=mesh['row'=4,'col'=8] {'row'}, dimensions={1}, use_global_device_ids=true | all-gather | bytes 491520 | tf_op jit(solution)/shard_map/all_gather | solution.py:23
  17.1 1.1 fusion.25
  18.2 27.2 %all_gather.7 = bf16[48,8192]{1,0:T(8,128)(2,1)S(1)} all-gather(bf16[48,1024]{1,0:T(8,128)(2,1)} %param.10), channel_id=1, replica_groups=mesh['row'=4,'col'=8] {'col'}, dimensions={1}, use_global_device_ids=true | all-gather | bytes 884736 | tf_op jit(solution)/shard_map/all_gather | solution.py:22
  45.4 0.7 compare_select_fusion
  46.0 0.7 compare_select_fusion.1
  46.7 29.3 %psum.14 = f32[48,48]{1,0:T(8,128)S(1)} all-reduce(f32[48,48]{1,0:T(8,128)S(1)} %fusion.25), channel_id=1, replica_groups=mesh['row'=4,'col'=8] {'col'}, use_global_device_ids=true, to_apply=%region_0.0 | all-reduce | flops 2304 | bytes 18432 | tf_op jit(solution)/shard_map/psum | solution.py:15
  76.0 23.1 %psum.15 = f32[48,48]{1,0:T(8,128)S(1)} all-reduce(f32[48,48]{1,0:T(8,128)S(1)} %fusion.26), channel_id=1, replica_groups=mesh['row'=4,'col'=8] {'row'}, use_global_device_ids=true, to_apply=%region_1.0 | all-reduce | flops 2304 | bytes 18432 | tf_op jit(solution)/shard_map/psum | solution.py:18
  99.1 0.1 copy.18
  99.2 4.4 %cholesky.16 = f32[48,48]{1,0:T(8,128)S(1)} custom-call(f32[48,48]{1,0:T(8,128)S(1)} %fusion.17), custom_call_target="Cholesky" | custom-call | tf_op jit(solution)/shard_map/jit(cholesky)/cholesky | solution.py:54
  103.6 0.1 copy_bitcast_fusion.1
  103.7 0.1 copy_bitcast_fusion
  103.8 0.6 gather_fusion
  104.4 0.6 gather_fusion.1
  104.9 12.1 %fusion.11 = f32[4,48,128,128]{3,1,2,0:T(8,128)} fusion(bf16[4,128,128,128]{3,2,1,0:T(8,128)(2,1)} %param.6, bf16[4,48,128]{2,1,0:T(8,128)(2,1)S(1)} %gather_fusion), kind=kOutput, calls=%fused_computation.15 | convolution fusion | flops 805306368 | bytes 29409280 | tf_op jit(solution)/shard_map/trc,tabc->trab/dot_general | solution.py:30
  117.0 16.6 %fusion = f32[4,48,1,128]{3,2,1,0:T(1,128)S(1)} fusion(f32[4,48,128,128]{3,1,2,0:T(8,128)} %fusion.11, bf16[4,48,128,1]{2,1,0,3:T(8,128)(2,1)S(1)} %bitcast.50), kind=kOutput, calls=%fused_computation.2 | convolution fusion | flops 37748736 | bytes 12730368 | tf_op jit(solution)/shard_map/trab,trb->tra/dot_general | solution.py:33
  133.6 0.4 fusion.7
  134.0 0.7 copy.22
  134.7 0.0 all-to-all-done
  134.7 3.4 %all-to-all-start.1 = ((f32[8,48,128]{2,1,0:T(8,128)}), f32[8,48,128]{2,1,0:T(8,128)S(1)}, u32[]{:S(2)}, u32[]{:S(2)}) async-start(f32[8,48,128]{2,1,0:T(8,128)} %copy.22), calls=%async_computation.1 | async-start | bytes 393216 | tf_op jit(solution)/shard_map/all_to_all | solution.py:46
  138.2 0.7 compare_reduce_fusion
  138.9 0.7 fusion.13
  139.6 3.7 %custom-call.8 = f32[1,48,48]{1,2,0:T(8,128)S(1)} custom-call(f32[1,48,48]{2,1,0:T(8,128)S(1)} %fusion.13), custom_call_target="InvertDiagBlocksLowerTriangular" | custom-call | tf_op jit(solution)/shard_map/triangular_solve | solution.py:56
  143.2 0.2 reduce.6
  143.5 1.3 all-to-all-done.1
  144.8 0.3 fusion.5
  145.0 0.4 fusion.2
  145.4 1.0 fusion.14
  (6 shorter events, 0.1 us)
Async XLA Ops:
  2.1 132.6 %all-to-all-start = ((s32[8,1,1]{2,1,0:T(1,128)}), s32[8,1,1]{2,1,0:T(1,128)S(1)}, u32[]{:S(2)}, u32[]{:S(2)}) async-start(s32[8,1,1]{2,1,0:T(1,128)} %copy.19), calls=%async_computation | async-start | bytes 8192 | tf_op jit(solution)/shard_map/all_to_all | solution.py:47
  134.7 10.0 %all-to-all-start.1 = ((f32[8,48,128]{2,1,0:T(8,128)}), f32[8,48,128]{2,1,0:T(8,128)S(1)}, u32[]{:S(2)}, u32[]{:S(2)}) async-start(f32[8,48,128]{2,1,0:T(8,128)} %copy.22), calls=%async_computation.1 | async-start | bytes 393216 | tf_op jit(solution)/shard_map/all_to_all | solution.py:46
where the time goes:
time: 149 us; the launch traced here: 146 us
  blocking collectives  87 us (58%)
  matrix products  32.9 us (22%)
  other arithmetic  12.5 us (8%)
  starting transfers between devices  9.75 us (7%)
  local copies, waits for them, and re-layouts  2.79 us (2%)
    psum x1, blocking collectives, body(): lax.psum(jnp.dot(factor_mode2, factor_mode2.T, preferred_element_type=jnp...  29.3 us
    all_gather x1, blocking collectives, body(): full_two = lax.all_gather(factor_mode2, 'col', axis=1, tiled=True)  27.2 us
    psum x1, blocking collectives, body(): lax.psum(jnp.dot(factor_mode3, factor_mode3.T, preferred_element_type=jnp...  23.1 us
    dot_general x1, matrix products, body(): jnp.einsum('trab,trb->tra', contracted, mode2_rows.astype(jnp.float32), p...  16.6 us
    dot_general x1, matrix products, body(): jnp.einsum('trc,tabc->trab', mode3_rows, tensor_tiles, preferred_element_...  12.1 us
    all_gather x1, blocking collectives, body(): full_three = lax.all_gather(factor_mode3, 'row', axis=1, tiled=True)  7.49 us
    all_to_all x1, starting transfers between devices, body(): lax.all_to_all(outgoing_ids, 'col', split_axis=0, concat_axis=0, tiled=True)  6.35 us
    another operation x3, other arithmetic, body(): cholesky_factor = jnp.linalg.cholesky(system)  5.13 us
  transfers between devices with their start and end apart: 2, of which 1 were waited for; matrix products, arithmetic and copies ran while one was open for 30% of the time, Pallas kernels for 0%

commit v1 on v0

v1 whole, which is shorter than its diff:
```python
import functools

import jax
import jax.numpy as jnp
from jax import lax
from jax.experimental import pallas as pl
from jax.experimental.pallas import tpu as pltpu
from jax.sharding import PartitionSpec as P

IB_DEV = 8
CORES = 2
MESH = pl.DeviceIdType.MESH
ridge_term = 0.5


def kernel(
    rows, hi, lo, chunk,
    id1, id2, id3, x_ref, f2_ref, f3_ref, out_ref,
    xv, f2g, f3g, weights, scale, sums, slots, landed,
    x_sem, own_sem, a_send, a_recv, b_send, b_recv, c_send, c_recv,
    d_send, d_recv, e_send, e_recv, s_send, s_recv,
):
    cols = hi * lo
    ny = rows // CORES
    tiles, edge = x_ref.shape[0], x_ref.shape[1]
    rank = f2_ref.shape[0]
    two_blocks = f2_ref.shape[1] // edge
    half = two_blocks // CORES
    three_blocks = f3_ref.shape[1] // edge
    me_r, me_c = lax.axis_index("row"), lax.axis_index("col")
    my_hi, my_lo = me_c // lo, lax.rem(me_c, lo)
    my_y, core = me_r // CORES, lax.rem(me_r, CORES)
    sibling = (me_r + 1 - 2 * core, me_c)

    local = []
    for ref, held, base, count in (
        (f2_ref, f2g, me_c * two_blocks, two_blocks),
        (f3_ref, f3g, me_r * three_blocks, three_blocks),
    ):
        for b in range(count):
            local.append(
                pltpu.make_async_copy(
                    ref.at[:, b * edge : (b + 1) * edge], held.at[base + b], own_sem.at[len(local)]
                )
            )
    loads = [pltpu.make_async_copy(x_ref.at[t], xv.at[t], x_sem.at[t]) for t in range(tiles)]
    for copy in local + loads:
        copy.start()

    barrier = pltpu.get_barrier_semaphore()
    partners = [(me_r, lax.rem(me_c + i, cols)) for i in range(1, cols)]
    partners.append(sibling)
    for i in range(1, ny):
        partners.append((lax.rem(my_y + i, ny) * CORES + core, me_c))
    for partner in partners:
        pl.semaphore_signal(barrier, inc=1, device_id=partner, device_id_type=MESH)
    for copy in local:
        copy.wait()
    pl.semaphore_wait(barrier, len(partners))

    sent = []

    def send(src, dst, send_sem, recv_sem, device):
        copy = pltpu.make_async_remote_copy(
            src_ref=src, dst_ref=dst, send_sem=send_sem, recv_sem=recv_sem,
            device_id=device, device_id_type=MESH,
        )
        copy.start()
        sent.append(copy)
        return copy

    def source_col(i, j):
        return lax.rem(my_hi - i + hi, hi) * lo + lax.rem(my_lo - j + lo, lo)

    def piece(col):
        return f2g.at[pl.ds(col * two_blocks + core * half, half)]

    def shard(row):
        return f3g.at[pl.ds(row * three_blocks, three_blocks)]

    mine, mine3 = piece(me_c), shard(me_r)
    a_copies, b_copies, c_copies, d_copies, e_copies = {}, {}, {}, {}, {}
    for i in range(1, hi):
        peer = (me_r, lax.rem(my_hi + i, hi) * lo + my_lo)
        a_copies[i] = send(mine, mine, a_send.at[i], a_recv.at[i], peer)

    def to_lo(i):
        where = piece(source_col(i, 0))
        for j in range(1, lo):
            peer = (me_r, my_hi * lo + lax.rem(my_lo + j, lo))
            b_copies[i, j] = send(where, where, b_send.at[i, j], b_recv.at[i, j], peer)

    def to_sibling(i, j):
        where = piece(source_col(i, j))
        c_copies[i, j] = send(where, where, c_send.at[i, j], c_recv.at[i, j], sibling)

    to_lo(0)
    for i in range(1, ny):
        peer = (lax.rem(my_y + i, ny) * CORES + core, me_c)
        e_copies[i] = send(mine3, mine3, e_send.at[i], e_recv.at[i], peer)
    d_copies[0] = send(mine3, mine3, d_send.at[0], d_recv.at[0], sibling)
    for i in range(1, hi):
        a_copies[i].wait_recv()
        to_lo(i)
        to_sibling(i, 0)
        for j in range(1, lo):
            b_copies[i - 1, j].wait_recv()
            to_sibling(i - 1, j)
    for i in range(1, ny):
        e_copies[i].wait_recv()
        where = shard(lax.rem(my_y - i + ny, ny) * CORES + core)
        d_copies[i] = send(where, where, d_send.at[i], d_recv.at[i], sibling)
    for j in range(1, lo):
        b_copies[hi - 1, j].wait_recv()
        to_sibling(hi - 1, j)
    for copy in list(c_copies.values()) + list(d_copies.values()):
        copy.wait_recv()

    for t in range(tiles):
        pair, side = t // 2, t % 2
        block = f3g[id3[t]].astype(jnp.float32)
        before = jnp.zeros((side * rank, edge), jnp.float32)
        after = jnp.zeros((edge - (side + 1) * rank, edge), jnp.float32)
        stacked = jnp.concatenate(([before] if side else []) + [block, after], axis=0)
        weights[pair, pl.ds(side * edge, edge), :] = stacked.T.astype(jnp.bfloat16)
    for pair in range(tiles // 2):
        blocks = [f2g[id2[t]].astype(jnp.float32) for t in (2 * pair, 2 * pair + 1)]
        blocks.append(jnp.zeros((edge - 2 * rank, edge), jnp.float32))
        scale[pair] = jnp.concatenate(blocks, axis=0).T

    for pair in range(tiles // 2):
        loads[2 * pair].wait()
        loads[2 * pair + 1].wait()

        def contract(step, _, pair=pair):
            at = pl.ds(pl.multiple_of(step * chunk, chunk), chunk)
            left = jnp.concatenate(
                [xv[2 * pair + s, at].reshape(chunk * edge, edge) for s in range(2)], axis=1
            )
            contracted = jnp.dot(left, weights[pair], preferred_element_type=jnp.float32)
            scaled = contracted.reshape(chunk, edge, edge) * scale[pair][None]
            sums[pair, at, :] = jnp.sum(scaled, axis=1)
            return 0

        lax.fori_loop(0, edge // chunk, contract, 0)

    tile_rows = []
    for pair in range(tiles // 2):
        turned = sums[pair].T
        tile_rows += [turned[:rank], turned[rank : 2 * rank]]
    row_blocks = IB_DEV * cols
    owners, within = [], []
    for t in range(tiles):
        block = jnp.full((rank, edge), id1[t]) - me_r * row_blocks
        owners.append(lax.div(block, jnp.int32(IB_DEV)))
        within.append(lax.rem(block[:1], jnp.int32(IB_DEV)))
    slot_copies = []
    for i in list(range(1, cols)) + [0]:
        to = lax.rem(me_c + i, cols)
        values = jnp.zeros((rank, edge), jnp.float32)
        ident = jnp.full((1, edge), -1, jnp.int32)
        for t in range(tiles):
            values = jnp.where(owners[t] == to, tile_rows[t], values)
            ident = jnp.where(owners[t][:1] == to, within[t], ident)
        target = slots if i else landed
        target[i, :rank, :] = values
        target[i, rank:, :] = jnp.broadcast_to(ident.astype(jnp.float32), (8, edge))
        if i:
            slot_copies.append(
                send(slots.at[i], landed.at[i], s_send.at[i], s_recv.at[i], (me_r, to))
            )

    nt = (((1,), (1,)), ((), ()))

    def gram(held, count):
        total = jnp.zeros((rank, rank), jnp.float32)
        for b in range(0, count, 2):
            part = jnp.concatenate([held[b], held[b + 1]], axis=1)
            total += lax.dot_general(part, part, nt, preferred_element_type=jnp.float32)
        return total

    gram_two = gram(f2g, cols * two_blocks)
    gram_three = gram(f3g, rows * three_blocks)
    row_id = lax.broadcasted_iota(jnp.int32, (rank, edge), 0)
    lane_id = lax.broadcasted_iota(jnp.int32, (rank, edge), 1)
    system = gram_two * gram_three
    padded = jnp.concatenate([system, jnp.zeros((rank, edge - rank), jnp.float32)], axis=1)
    padded = padded + jnp.where(lane_id == row_id, ridge_term, 0.0)
    start = padded + jnp.where(lane_id == row_id + rank, 1.0, 0.0)

    def eliminate(k, work):
        row = jnp.sum(jnp.where(row_id == k, work, 0.0), axis=0, keepdims=True)
        col = jnp.sum(jnp.where(lane_id == k, work, 0.0), axis=1, keepdims=True)
        pivot = jnp.sum(jnp.where(lane_id[:1] == k, row, 0.0), axis=1, keepdims=True)
        row = row / pivot
        return jnp.where(row_id == k, row, work - col * row)

    inverse = lax.fori_loop(0, rank, eliminate, start)[:, rank : 2 * rank]

    for copy in slot_copies:
        copy.wait_recv()
    for b in range(IB_DEV):
        right = jnp.zeros((rank, edge), jnp.float32)
        for i in range(cols):
            right += jnp.where(landed[i, rank : rank + 1, :] == float(b), landed[i, :rank, :], 0.0)
        out_ref[:, b * edge : (b + 1) * edge] = jnp.dot(
            inverse, right, preferred_element_type=jnp.float32, precision=lax.Precision.HIGHEST
        )
    for copy in sent:
        copy.wait_send()


def solution(mesh):
    rows, cols = mesh.shape["row"], mesh.shape["col"]
    lo = 1
    while 4 * lo * lo <= cols:
        lo *= 2
    hi = cols // lo

    def body(tensor_tiles, tile_mode1, tile_mode2, tile_mode3, factor_mode2, factor_mode3):
        tiles, edge = tensor_tiles.shape[:2]
        rank = factor_mode2.shape[0]
        two_blocks = factor_mode2.shape[1] // edge
        three_blocks = factor_mode3.shape[1] // edge
        dma = pltpu.SemaphoreType.DMA
        smem = pl.BlockSpec(memory_space=pltpu.SMEM)
        hbm = pl.BlockSpec(memory_space=pl.ANY)
        return pl.pallas_call(
            functools.partial(kernel, rows, hi, lo, 16),
            out_shape=jax.ShapeDtypeStruct((rank, IB_DEV * edge), jnp.float32),
            in_specs=[smem, smem, smem, hbm, hbm, hbm],
            out_specs=pl.BlockSpec(memory_space=pltpu.VMEM),
            scratch_shapes=[
                pltpu.VMEM(tensor_tiles.shape, jnp.bfloat16),
                pltpu.VMEM((cols * two_blocks, rank, edge), jnp.bfloat16),
                pltpu.VMEM((rows * three_blocks, rank, edge), jnp.bfloat16),
                pltpu.VMEM((tiles // 2, 2 * edge, edge), jnp.bfloat16),
                pltpu.VMEM((tiles // 2, edge, edge), jnp.float32),
                pltpu.VMEM((tiles // 2, edge, edge), jnp.float32),
                pltpu.VMEM((cols, rank + 8, edge), jnp.float32),
                pltpu.VMEM((cols, rank + 8, edge), jnp.float32),
                dma((tiles,)),
                dma((two_blocks + three_blocks,)),
                dma((hi,)), dma((hi,)),
                dma((hi, lo)), dma((hi, lo)),
                dma((hi, lo)), dma((hi, lo)),
                dma((rows,)), dma((rows,)),
                dma((rows,)), dma((rows,)),
                dma((cols,)), dma((cols,)),
            ],
            compiler_params=pltpu.CompilerParams(
                collective_id=0, has_side_effects=True, vmem_limit_bytes=48 * 1024 * 1024
            ),
        )(tile_mode1, tile_mode2, tile_mode3, tensor_tiles, factor_mode2, factor_mode3)

    in_specs = (
        P(("row", "col"), None, None, None),
        P(("row", "col")),
        P(("row", "col")),
        P(("row", "col")),
        P(None, "col"),
        P(None, "row"),
    )
    out_specs = P(None, ("row", "col"))
    return jax.shard_map(body, mesh=mesh, in_specs=in_specs, out_specs=out_specs, check_vma=False)
```

time: 149 us -> 35.9 us (0.24); the launches traced: 146 us -> 35.7 us
  blocking collectives: 87 us -> 0 us
  matrix products: 32.9 us -> 0 us
  Pallas kernels: 0 us -> 31.2 us
  other arithmetic: 12.5 us -> 0 us
  starting transfers between devices: 9.75 us -> 0 us
  local copies, waits for them, and re-layouts: 2.79 us -> 4.43 us
    psum x2 -> x0, blocking collectives: 52.4 us -> none  [the longest x1 29.3 us: body(): lax.psum(jnp.dot(factor_mode2, factor_mode2.T, preferred_element_type=jnp...]
    all_gather x2 -> x0, blocking collectives: 34.6 us -> none  [the longest x1 27.2 us: body(): full_two = lax.all_gather(factor_mode2, 'col', axis=1, tiled=True)]
    dot_general x6 -> x0, matrix products: 31.6 us -> none  [the longest x1 16.6 us: body(): jnp.einsum('trab,trb->tra', contracted, mode2_rows.astype(jnp.float32), p...]
    pallas_call x0 -> x1, Pallas kernels: none -> 31.2 us  [body(): pl.pallas_call(functools.partial(kernel, rows, hi, lo, 16), out_shape=jax...]
    all_to_all x2 -> x0, starting transfers between devices: 9.75 us -> none  [the longest x1 6.35 us: body(): lax.all_to_all(outgoing_ids, 'col', split_axis=0, concat_axis=0, tiled=True)]
    another operation x5 -> x0, other arithmetic: 9.49 us -> none  [the longest x3 5.13 us: body(): cholesky_factor = jnp.linalg.cholesky(system)]
    unnamed x0 -> x11, local copies, waits for them, and re-layouts: none -> 4.43 us
    select_n x3 -> x0, other arithmetic: 1.98 us -> none  [the longest x1 0.66 us: body(): owner_slot = local_blocks // IB_DEV]
  transfers between devices with their start and end apart: 2 -> 0, of which waited for: 1 -> 0; matrix products, arithmetic and copies ran while one was open for 30% -> 0% of each run, Pallas kernels for 0% -> 0%
where the time goes in v1:
time: 35.9 us; the launch traced here: 35.7 us
  Pallas kernels  31.2 us (87%)
  local copies, waits for them, and re-layouts  4.43 us (12%)
    pallas_call x1, Pallas kernels, body(): pl.pallas_call(functools.partial(kernel, rows, hi, lo, 16), out_shape=jax...  31.2 us
    unnamed x11, local copies, waits for them, and re-layouts  4.43 us

profile of v1, /device:TPU:1, one launch (start us, length us, event | category | flops | bytes accessed | tf_op | source)
XLA Modules:
  0.0 35.7 jit_solution(11842191335055160621)
XLA Ops:
  0.0 0.0 copy-start
  0.0 0.9 %copy-done = bf16[48,1024]{1,0:T(8,128)(2,1)S(1)} copy-done((bf16[48,1024]{1,0:T(8,128)(2,1)S(1)}, bf16[48,1024]{1,0:T(8,128)(2,1)}, u32[]{:S(2)}) %copy-start) | copy-done | bytes 98328
  0.9 0.0 copy-start.1
  0.9 0.9 %copy-done.1 = bf16[48,1024]{1,0:T(8,128)(2,1)S(1)} copy-done((bf16[48,1024]{1,0:T(8,128)(2,1)S(1)}, bf16[48,1024]{1,0:T(8,128)(2,1)}, u32[]{:S(2)}) %copy-start.1) | copy-done | bytes 98328
  1.8 0.0 copy-start.2
  1.8 0.7 %copy-done.2 = s32[4]{0:T(128)S(1)} copy-done((s32[4]{0:T(128)S(1)}, s32[4]{0:T(128)}, u32[]{:S(2)}) %copy-start.2) | copy-done | bytes 40
  2.4 0.0 copy-start.3
  2.4 0.7 %copy-done.3 = s32[4]{0:T(128)S(1)} copy-done((s32[4]{0:T(128)S(1)}, s32[4]{0:T(128)}, u32[]{:S(2)}) %copy-start.3) | copy-done | bytes 40
  3.1 0.0 copy-start.4
  3.1 0.7 %copy-done.4 = s32[4]{0:T(128)S(1)} copy-done((s32[4]{0:T(128)S(1)}, s32[4]{0:T(128)}, u32[]{:S(2)}) %copy-start.4) | copy-done | bytes 40
  3.8 31.2 %shard_map.64 = f32[48,1024]{1,0:T(8,128)S(1)} custom-call(s32[4]{0:T(128)S(1)} %copy-done.2, s32[4]{0:T(128)S(1)} %copy-done.3, s32[4]{0:T(128)S(1)} %copy-done.4, bf16[4,128,128,128]{3,2,1,0:T(8,128)(2,1)} %x_ref.1, bf16[48,1024]{1,0:T(8,128)(2,1)S(1)} %copy-done, bf16[48,1024]{1,0:T(8,128)(2,1)S(1)} %copy-done.1), custom_call_target="tpu_custom_call" | custom-call | tf_op jit(solution)/shard_map/pallas_call | solution.py:228
  35.0 0.7 %copy.8 = f32[48,1024]{1,0:T(8,128)} copy(f32[48,1024]{1,0:T(8,128)S(1)} %shard_map.64) | data formatting | bytes 393216
Async XLA Ops:
  0.0 0.9 %copy-start = (bf16[48,1024]{1,0:T(8,128)(2,1)S(1)}, bf16[48,1024]{1,0:T(8,128)(2,1)}, u32[]{:S(2)}) copy-start(bf16[48,1024]{1,0:T(8,128)(2,1)} %f2_ref.1) | copy-start | bytes 294916
  0.9 0.9 %copy-start.1 = (bf16[48,1024]{1,0:T(8,128)(2,1)S(1)}, bf16[48,1024]{1,0:T(8,128)(2,1)}, u32[]{:S(2)}) copy-start(bf16[48,1024]{1,0:T(8,128)(2,1)} %f3_ref.1) | copy-start | bytes 294916
  1.8 0.7 %copy-start.2 = (s32[4]{0:T(128)S(1)}, s32[4]{0:T(128)}, u32[]{:S(2)}) copy-start(s32[4]{0:T(128)} %id1.1) | copy-start | bytes 52
  2.4 0.7 %copy-start.3 = (s32[4]{0:T(128)S(1)}, s32[4]{0:T(128)}, u32[]{:S(2)}) copy-start(s32[4]{0:T(128)} %id2.1) | copy-start | bytes 52
  3.1 0.7 %copy-start.4 = (s32[4]{0:T(128)S(1)}, s32[4]{0:T(128)}, u32[]{:S(2)}) copy-start(s32[4]{0:T(128)} %id3.1) | copy-start | bytes 52

commit v2 on v1

--- a/solution.py
+++ b/solution.py
@@ -15,9 +15,9 @@
 
 def kernel(
     rows, hi, lo, chunk,
-    id1, id2, id3, x_ref, f2_ref, f3_ref, out_ref,
-    xv, f2g, f3g, weights, scale, sums, slots, landed,
-    x_sem, own_sem, a_send, a_recv, b_send, b_recv, c_send, c_recv,
+    id1_ref, id2_ref, id3_ref, x_ref, f2_ref, f3_ref, out_ref,
+    id1, id2, id3, xv, f2g, f3g, weights, scale, sums, slots, landed,
+    id_sem, x_sem, own_sem, a_send, a_recv, b_send, b_recv, c_send, c_recv,
     d_send, d_recv, e_send, e_recv, s_send, s_recv,
 ):
     cols = hi * lo
@@ -44,7 +44,11 @@
                 )
             )
     loads = [pltpu.make_async_copy(x_ref.at[t], xv.at[t], x_sem.at[t]) for t in range(tiles)]
-    for copy in local + loads:
+    ids = [
+        pltpu.make_async_copy(ref, held, id_sem.at[n])
+        for n, (ref, held) in enumerate(((id1_ref, id1), (id2_ref, id2), (id3_ref, id3)))
+    ]
+    for copy in local + ids + loads:
         copy.start()
 
     barrier = pltpu.get_barrier_semaphore()
@@ -54,7 +58,7 @@
         partners.append((lax.rem(my_y + i, ny) * CORES + core, me_c))
     for partner in partners:
         pl.semaphore_signal(barrier, inc=1, device_id=partner, device_id_type=MESH)
-    for copy in local:
+    for copy in local + ids:
         copy.wait()
     pl.semaphore_wait(barrier, len(partners))
 
@@ -94,11 +98,29 @@
         where = piece(source_col(i, j))
         c_copies[i, j] = send(where, where, c_send.at[i, j], c_recv.at[i, j], sibling)
 
+    grams = [jnp.zeros((rank, rank), jnp.float32) for _ in range(2)]
+
+    def add_gram(which, held, base, count):
+        for b in range(0, count, 2):
+            part = jnp.concatenate([held[base + b], held[base + b + 1]], axis=1)
+            grams[which] += lax.dot_general(
+                part, part, (((1,), (1,)), ((), ())), preferred_element_type=jnp.float32
+            )
+
+    def add_piece(i, j, side):
+        add_gram(0, f2g, source_col(i, j) * two_blocks + side * half, half)
+
+    def add_shard(row):
+        add_gram(1, f3g, row * three_blocks, three_blocks)
+
     to_lo(0)
     for i in range(1, ny):
         peer = (lax.rem(my_y + i, ny) * CORES + core, me_c)
         e_copies[i] = send(mine3, mine3, e_send.at[i], e_recv.at[i], peer)
     d_copies[0] = send(mine3, mine3, d_send.at[0], d_recv.at[0], sibling)
+    add_piece(0, 0, 0)
+    add_piece(0, 0, 1)
+    add_shard(me_r)
     for i in range(1, hi):
         a_copies[i].wait_recv()
         to_lo(i)
@@ -106,15 +128,24 @@
         for j in range(1, lo):
             b_copies[i - 1, j].wait_recv()
             to_sibling(i - 1, j)
+        add_piece(i, 0, core)
+        for j in range(1, lo):
+            add_piece(i - 1, j, core)
     for i in range(1, ny):
         e_copies[i].wait_recv()
         where = shard(lax.rem(my_y - i + ny, ny) * CORES + core)
         d_copies[i] = send(where, where, d_send.at[i], d_recv.at[i], sibling)
+        add_shard(lax.rem(my_y - i + ny, ny) * CORES + core)
     for j in range(1, lo):
         b_copies[hi - 1, j].wait_recv()
         to_sibling(hi - 1, j)
-    for copy in list(c_copies.values()) + list(d_copies.values()):
-        copy.wait_recv()
+        add_piece(hi - 1, j, core)
+    for i in range(ny):
+        d_copies[i].wait_recv()
+        add_shard(lax.rem(my_y - i + ny, ny) * CORES + 1 - core)
+    for i, j in c_copies:
+        c_copies[i, j].wait_recv()
+        add_piece(i, j, 1 - core)
 
     for t in range(tiles):
         pair, side = t // 2, t % 2
@@ -170,32 +201,25 @@
                 send(slots.at[i], landed.at[i], s_send.at[i], s_recv.at[i], (me_r, to))
             )
 
-    nt = (((1,), (1,)), ((), ()))
-
-    def gram(held, count):
-        total = jnp.zeros((rank, rank), jnp.float32)
-        for b in range(0, count, 2):
-            part = jnp.concatenate([held[b], held[b + 1]], axis=1)
-            total += lax.dot_general(part, part, nt, preferred_element_type=jnp.float32)
-        return total
-
-    gram_two = gram(f2g, cols * two_blocks)
-    gram_three = gram(f3g, rows * three_blocks)
     row_id = lax.broadcasted_iota(jnp.int32, (rank, edge), 0)
     lane_id = lax.broadcasted_iota(jnp.int32, (rank, edge), 1)
-    system = gram_two * gram_three
+    system = grams[0] * grams[1]
     padded = jnp.concatenate([system, jnp.zeros((rank, edge - rank), jnp.float32)], axis=1)
     padded = padded + jnp.where(lane_id == row_id, ridge_term, 0.0)
-    start = padded + jnp.where(lane_id == row_id + rank, 1.0, 0.0)
-
-    def eliminate(k, work):
-        row = jnp.sum(jnp.where(row_id == k, work, 0.0), axis=0, keepdims=True)
-        col = jnp.sum(jnp.where(lane_id == k, work, 0.0), axis=1, keepdims=True)
-        pivot = jnp.sum(jnp.where(lane_id[:1] == k, row, 0.0), axis=1, keepdims=True)
-        row = row / pivot
-        return jnp.where(row_id == k, row, work - col * row)
-
-    inverse = lax.fori_loop(0, rank, eliminate, start)[:, rank : 2 * rank]
+    work = padded + jnp.where(lane_id == row_id + rank, 1.0, 0.0)
+    for k in range(0, rank, 2):
+        first = jnp.broadcast_to(work[:, k : k + 1], (rank, edge))
+        second = jnp.broadcast_to(work[:, k + 1 : k + 2], (rank, edge))
+        row_a, row_b = work[k : k + 1], work[k + 1 : k + 2]
+        inv_a = 1.0 / first[k : k + 1]
+        cross = second[k : k + 1]
+        factor = first[k + 1 : k + 2] * inv_a
+        inv_b = 1.0 / (second[k + 1 : k + 2] - factor * cross)
+        new_b = (row_b - factor * row_a) * inv_b
+        new_a = (row_a - cross * new_b) * inv_a
+        work = work - first * new_a - second * new_b
+        work = jnp.where(row_id == k, new_a, jnp.where(row_id == k + 1, new_b, work))
+    inverse = work[:, rank : 2 * rank]
 
     for copy in slot_copies:
         copy.wait_recv()
@@ -223,14 +247,16 @@
         two_blocks = factor_mode2.shape[1] // edge
         three_blocks = factor_mode3.shape[1] // edge
         dma = pltpu.SemaphoreType.DMA
-        smem = pl.BlockSpec(memory_space=pltpu.SMEM)
-        hbm = pl.BlockSpec(memory_space=pl.ANY)
+        hbm = pl.BlockSpec(memory_space=pltpu.HBM)
         return pl.pallas_call(
             functools.partial(kernel, rows, hi, lo, 16),
             out_shape=jax.ShapeDtypeStruct((rank, IB_DEV * edge), jnp.float32),
-            in_specs=[smem, smem, smem, hbm, hbm, hbm],
+            in_specs=[hbm] * 6,
             out_specs=pl.BlockSpec(memory_space=pltpu.VMEM),
             scratch_shapes=[
+                pltpu.SMEM((tiles,), jnp.int32),
+                pltpu.SMEM((tiles,), jnp.int32),
+                pltpu.SMEM((tiles,), jnp.int32),
                 pltpu.VMEM(tensor_tiles.shape, jnp.bfloat16),
                 pltpu.VMEM((cols * two_blocks, rank, edge), jnp.bfloat16),
                 pltpu.VMEM((rows * three_blocks, rank, edge), jnp.bfloat16),
@@ -239,6 +265,7 @@
                 pltpu.VMEM((tiles // 2, edge, edge), jnp.float32),
                 pltpu.VMEM((cols, rank + 8, edge), jnp.float32),
                 pltpu.VMEM((cols, rank + 8, edge), jnp.float32),
+                dma((3,)),
                 dma((tiles,)),
                 dma((two_blocks + three_blocks,)),
                 dma((hi,)), dma((hi,)),
@@ -249,7 +276,7 @@
                 dma((cols,)), dma((cols,)),
             ],
             compiler_params=pltpu.CompilerParams(
-                collective_id=0, has_side_effects=True, vmem_limit_bytes=48 * 1024 * 1024
+                collective_id=0, has_side_effects=True, vmem_limit_bytes=60 * 1024 * 1024
             ),
         )(tile_mode1, tile_mode2, tile_mode3, tensor_tiles, factor_mode2, factor_mode3)
 

time: 35.9 us -> 38.6 us (1.075)
  Pallas kernels: 31.2 us -> 36.5 us
  local copies, waits for them, and re-layouts: 4.43 us -> 1.62 us
    pallas_call x1, Pallas kernels: 31.2 us -> 36.5 us  [body(): pl.pallas_call(functools.partial(kernel, rows, hi, lo, 16), out_shape=jax...]
    unnamed x11 -> x1, local copies, waits for them, and re-layouts: 4.43 us -> 1.62 us
where the time goes in v2:
time: 38.6 us; the launch traced here: 38.1 us
  Pallas kernels  36.5 us (95%)
  local copies, waits for them, and re-layouts  1.62 us (4%)
    pallas_call x1, Pallas kernels, body(): pl.pallas_call(functools.partial(kernel, rows, hi, lo, 16), out_shape=jax...  36.5 us
    unnamed x1, local copies, waits for them, and re-layouts  1.62 us

profile of v2, /device:TPU:1, one launch (start us, length us, event | category | flops | bytes accessed | tf_op | source)
XLA Modules:
  0.0 38.1 jit_solution(2336004263017103008)
XLA Ops:
  0.0 36.5 %shard_map.64 = f32[48,1024]{1,0:T(8,128)} custom-call(s32[4]{0:T(128)} %id1_ref.1, s32[4]{0:T(128)} %id2_ref.1, s32[4]{0:T(128)} %id3_ref.1, bf16[4,128,128,128]{3,2,1,0:T(8,128)(2,1)} %x_ref.1, bf16[48,1024]{1,0:T(8,128)(2,1)} %f2_ref.1, bf16[48,1024]{1,0:T(8,128)(2,1)} %f3_ref.1), custom_call_target="tpu_custom_call" | custom-call | tf_op jit(solution)/shard_map/pallas_call | solution.py:251
  36.5 1.6 %copy.8 = f32[48,1024]{1,0:T(8,128)} copy(f32[48,1024]{1,0:T(8,128)} %shard_map.64) | data formatting | bytes 393216

commit v3 on v2

--- a/solution.py
+++ b/solution.py
@@ -48,7 +48,7 @@
         pltpu.make_async_copy(ref, held, id_sem.at[n])
         for n, (ref, held) in enumerate(((id1_ref, id1), (id2_ref, id2), (id3_ref, id3)))
     ]
-    for copy in local + ids + loads:
+    for copy in local + ids:
         copy.start()
 
     barrier = pltpu.get_barrier_semaphore()
@@ -58,7 +58,7 @@
         partners.append((lax.rem(my_y + i, ny) * CORES + core, me_c))
     for partner in partners:
         pl.semaphore_signal(barrier, inc=1, device_id=partner, device_id_type=MESH)
-    for copy in local + ids:
+    for copy in local:
         copy.wait()
     pl.semaphore_wait(barrier, len(partners))
 
@@ -98,29 +98,13 @@
         where = piece(source_col(i, j))
         c_copies[i, j] = send(where, where, c_send.at[i, j], c_recv.at[i, j], sibling)
 
-    grams = [jnp.zeros((rank, rank), jnp.float32) for _ in range(2)]
-
-    def add_gram(which, held, base, count):
-        for b in range(0, count, 2):
-            part = jnp.concatenate([held[base + b], held[base + b + 1]], axis=1)
-            grams[which] += lax.dot_general(
-                part, part, (((1,), (1,)), ((), ())), preferred_element_type=jnp.float32
-            )
-
-    def add_piece(i, j, side):
-        add_gram(0, f2g, source_col(i, j) * two_blocks + side * half, half)
-
-    def add_shard(row):
-        add_gram(1, f3g, row * three_blocks, three_blocks)
-
     to_lo(0)
     for i in range(1, ny):
         peer = (lax.rem(my_y + i, ny) * CORES + core, me_c)
         e_copies[i] = send(mine3, mine3, e_send.at[i], e_recv.at[i], peer)
     d_copies[0] = send(mine3, mine3, d_send.at[0], d_recv.at[0], sibling)
-    add_piece(0, 0, 0)
-    add_piece(0, 0, 1)
-    add_shard(me_r)
+    for copy in loads:
+        copy.start()
     for i in range(1, hi):
         a_copies[i].wait_recv()
         to_lo(i)
@@ -128,24 +112,17 @@
         for j in range(1, lo):
             b_copies[i - 1, j].wait_recv()
             to_sibling(i - 1, j)
-        add_piece(i, 0, core)
-        for j in range(1, lo):
-            add_piece(i - 1, j, core)
     for i in range(1, ny):
         e_copies[i].wait_recv()
         where = shard(lax.rem(my_y - i + ny, ny) * CORES + core)
         d_copies[i] = send(where, where, d_send.at[i], d_recv.at[i], sibling)
-        add_shard(lax.rem(my_y - i + ny, ny) * CORES + core)
     for j in range(1, lo):
         b_copies[hi - 1, j].wait_recv()
         to_sibling(hi - 1, j)
-        add_piece(hi - 1, j, core)
-    for i in range(ny):
-        d_copies[i].wait_recv()
-        add_shard(lax.rem(my_y - i + ny, ny) * CORES + 1 - core)
-    for i, j in c_copies:
-        c_copies[i, j].wait_recv()
-        add_piece(i, j, 1 - core)
+    for copy in list(c_copies.values()) + list(d_copies.values()):
+        copy.wait_recv()
+    for copy in ids:
+        copy.wait()
 
     for t in range(tiles):
         pair, side = t // 2, t % 2
@@ -201,9 +178,18 @@
                 send(slots.at[i], landed.at[i], s_send.at[i], s_recv.at[i], (me_r, to))
             )
 
+    def gram(held, count):
+        total = jnp.zeros((rank, rank), jnp.float32)
+        for base in range(0, count, 16):
+            part = jnp.concatenate([held[b] for b in range(base, min(base + 16, count))], axis=1)
+            total += lax.dot_general(
+                part, part, (((1,), (1,)), ((), ())), preferred_element_type=jnp.float32
+            )
+        return total
+
     row_id = lax.broadcasted_iota(jnp.int32, (rank, edge), 0)
     lane_id = lax.broadcasted_iota(jnp.int32, (rank, edge), 1)
-    system = grams[0] * grams[1]
+    system = gram(f2g, cols * two_blocks) * gram(f3g, rows * three_blocks)
     padded = jnp.concatenate([system, jnp.zeros((rank, edge - rank), jnp.float32)], axis=1)
     padded = padded + jnp.where(lane_id == row_id, ridge_term, 0.0)
     work = padded + jnp.where(lane_id == row_id + rank, 1.0, 0.0)

time: 38.6 us -> 33 us (0.85)
  Pallas kernels: 36.5 us -> 31.2 us
    pallas_call x1, Pallas kernels: 36.5 us -> 31.2 us  [body(): pl.pallas_call(functools.partial(kernel, rows, hi, lo, 16), out_shape=jax...]
where the time goes in v3:
time: 33 us; the launch traced here: 32.8 us
  Pallas kernels  31.2 us (95%)
  local copies, waits for them, and re-layouts  1.62 us (5%)
    pallas_call x1, Pallas kernels, body(): pl.pallas_call(functools.partial(kernel, rows, hi, lo, 16), out_shape=jax...  31.2 us
    unnamed x1, local copies, waits for them, and re-layouts  1.62 us

profile of v3, /device:TPU:1, one launch (start us, length us, event | category | flops | bytes accessed | tf_op | source)
XLA Modules:
  0.0 32.8 jit_solution(8297154353916490688)
XLA Ops:
  0.0 31.2 %shard_map.64 = f32[48,1024]{1,0:T(8,128)} custom-call(s32[4]{0:T(128)} %id1_ref.1, s32[4]{0:T(128)} %id2_ref.1, s32[4]{0:T(128)} %id3_ref.1, bf16[4,128,128,128]{3,2,1,0:T(8,128)(2,1)} %x_ref.1, bf16[48,1024]{1,0:T(8,128)(2,1)} %f2_ref.1, bf16[48,1024]{1,0:T(8,128)(2,1)} %f3_ref.1), custom_call_target="tpu_custom_call" | custom-call | tf_op jit(solution)/shard_map/pallas_call | solution.py:237
  31.2 1.6 %copy.8 = f32[48,1024]{1,0:T(8,128)} copy(f32[48,1024]{1,0:T(8,128)} %shard_map.64) | data formatting | bytes 393216

commit v4 on v3

--- a/solution.py
+++ b/solution.py
@@ -16,7 +16,7 @@
 def kernel(
     rows, hi, lo, chunk,
     id1_ref, id2_ref, id3_ref, x_ref, f2_ref, f3_ref, out_ref,
-    id1, id2, id3, xv, f2g, f3g, weights, scale, sums, slots, landed,
+    id1, id2, id3, xv, f2g, f3g, weights, scale, sums, slots_a, slots_b, landed_a, landed_b,
     id_sem, x_sem, own_sem, a_send, a_recv, b_send, b_recv, c_send, c_recv,
     d_send, d_recv, e_send, e_recv, s_send, s_recv,
 ):
@@ -136,47 +136,57 @@
         blocks.append(jnp.zeros((edge - 2 * rank, edge), jnp.float32))
         scale[pair] = jnp.concatenate(blocks, axis=0).T
 
-    for pair in range(tiles // 2):
-        loads[2 * pair].wait()
-        loads[2 * pair + 1].wait()
-
-        def contract(step, _, pair=pair):
-            at = pl.ds(pl.multiple_of(step * chunk, chunk), chunk)
-            left = jnp.concatenate(
-                [xv[2 * pair + s, at].reshape(chunk * edge, edge) for s in range(2)], axis=1
-            )
-            contracted = jnp.dot(left, weights[pair], preferred_element_type=jnp.float32)
-            scaled = contracted.reshape(chunk, edge, edge) * scale[pair][None]
-            sums[pair, at, :] = jnp.sum(scaled, axis=1)
-            return 0
-
-        lax.fori_loop(0, edge // chunk, contract, 0)
-
-    tile_rows = []
-    for pair in range(tiles // 2):
-        turned = sums[pair].T
-        tile_rows += [turned[:rank], turned[rank : 2 * rank]]
     row_blocks = IB_DEV * cols
+    half_rank, half_edge = rank // 2, edge // 2
     owners, within = [], []
     for t in range(tiles):
-        block = jnp.full((rank, edge), id1[t]) - me_r * row_blocks
+        block = jnp.full((half_rank, edge), id1[t]) - me_r * row_blocks
         owners.append(lax.div(block, jnp.int32(IB_DEV)))
         within.append(lax.rem(block[:1], jnp.int32(IB_DEV)))
+
     slot_copies = []
-    for i in list(range(1, cols)) + [0]:
-        to = lax.rem(me_c + i, cols)
-        values = jnp.zeros((rank, edge), jnp.float32)
-        ident = jnp.full((1, edge), -1, jnp.int32)
-        for t in range(tiles):
-            values = jnp.where(owners[t] == to, tile_rows[t], values)
-            ident = jnp.where(owners[t][:1] == to, within[t], ident)
-        target = slots if i else landed
-        target[i, :rank, :] = values
-        target[i, rank:, :] = jnp.broadcast_to(ident.astype(jnp.float32), (8, edge))
-        if i:
-            slot_copies.append(
-                send(slots.at[i], landed.at[i], s_send.at[i], s_recv.at[i], (me_r, to))
-            )
+    steps = half_edge // chunk
+    for part, (slots, landed) in enumerate(((slots_a, landed_a), (slots_b, landed_b))):
+        packed = []
+        for pair in range(tiles // 2):
+            if part == 0:
+                loads[2 * pair].wait()
+                loads[2 * pair + 1].wait()
+
+            def contract(step, _, pair=pair):
+                at = pl.ds(pl.multiple_of(step * chunk, chunk), chunk)
+                left = jnp.concatenate(
+                    [xv[2 * pair + s, at].reshape(chunk * edge, edge) for s in range(2)], axis=1
+                )
+                contracted = jnp.dot(left, weights[pair], preferred_element_type=jnp.float32)
+                scaled = contracted.reshape(chunk, edge, edge) * scale[pair][None]
+                sums[pair, at, :] = jnp.sum(scaled, axis=1)
+                return 0
+
+            lax.fori_loop(part * steps, (part + 1) * steps, contract, 0, unroll=2)
+            turned = sums[pair, part * half_edge : (part + 1) * half_edge, :].T
+            for s in range(2):
+                top = turned[s * rank : s * rank + half_rank]
+                low = turned[s * rank + half_rank : (s + 1) * rank]
+                packed.append(jnp.concatenate([top, low], axis=1))
+        for i in list(range(1, cols)) + [0]:
+            to = lax.rem(me_c + i, cols)
+            values = jnp.zeros((half_rank, edge), jnp.float32)
+            for t in range(tiles):
+                values = jnp.where(owners[t] == to, packed[t], values)
+            target = slots if i else landed
+            target[i, :half_rank, :] = values
+            if part == 0:
+                ident = jnp.full((1, edge), -1, jnp.int32)
+                for t in range(tiles):
+                    ident = jnp.where(owners[t][:1] == to, within[t], ident)
+                target[i, half_rank:, :] = jnp.broadcast_to(ident.astype(jnp.float32), (8, edge))
+            if i:
+                slot_copies.append(
+                    send(
+                        slots.at[i], landed.at[i], s_send.at[part, i], s_recv.at[part, i], (me_r, to)
+                    )
+                )
 
     def gram(held, count):
         total = jnp.zeros((rank, rank), jnp.float32)
@@ -210,11 +220,17 @@
     for copy in slot_copies:
         copy.wait_recv()
     for b in range(IB_DEV):
-        right = jnp.zeros((rank, edge), jnp.float32)
+        first = jnp.zeros((half_rank, edge), jnp.float32)
+        second = jnp.zeros((half_rank, edge), jnp.float32)
         for i in range(cols):
-            right += jnp.where(landed[i, rank : rank + 1, :] == float(b), landed[i, :rank, :], 0.0)
+            hit = landed_a[i, half_rank : half_rank + 1, :] == float(b)
+            first += jnp.where(hit, landed_a[i, :half_rank, :], 0.0)
+            second += jnp.where(hit, landed_b[i, :half_rank, :], 0.0)
+        top = jnp.concatenate([first[:, :half_edge], second[:, :half_edge]], axis=1)
+        low = jnp.concatenate([first[:, half_edge:], second[:, half_edge:]], axis=1)
         out_ref[:, b * edge : (b + 1) * edge] = jnp.dot(
-            inverse, right, preferred_element_type=jnp.float32, precision=lax.Precision.HIGHEST
+            inverse, jnp.concatenate([top, low], axis=0),
+            preferred_element_type=jnp.float32, precision=lax.Precision.HIGHEST,
         )
     for copy in sent:
         copy.wait_send()
@@ -249,8 +265,10 @@
                 pltpu.VMEM((tiles // 2, 2 * edge, edge), jnp.bfloat16),
                 pltpu.VMEM((tiles // 2, edge, edge), jnp.float32),
                 pltpu.VMEM((tiles // 2, edge, edge), jnp.float32),
-                pltpu.VMEM((cols, rank + 8, edge), jnp.float32),
-                pltpu.VMEM((cols, rank + 8, edge), jnp.float32),
+                pltpu.VMEM((cols, rank // 2 + 8, edge), jnp.float32),
+                pltpu.VMEM((cols, rank // 2, edge), jnp.float32),
+                pltpu.VMEM((cols, rank // 2 + 8, edge), jnp.float32),
+                pltpu.VMEM((cols, rank // 2, edge), jnp.float32),
                 dma((3,)),
                 dma((tiles,)),
                 dma((two_blocks + three_blocks,)),
@@ -259,7 +277,7 @@
                 dma((hi, lo)), dma((hi, lo)),
                 dma((rows,)), dma((rows,)),
                 dma((rows,)), dma((rows,)),
-                dma((cols,)), dma((cols,)),
+                dma((2, cols)), dma((2, cols)),
             ],
             compiler_params=pltpu.CompilerParams(
                 collective_id=0, has_side_effects=True, vmem_limit_bytes=60 * 1024 * 1024

time: 33 us -> 30.6 us (0.927)
  Pallas kernels: 31.2 us -> 28.8 us
    pallas_call x1, Pallas kernels: 31.2 us -> 28.8 us  [body(): pl.pallas_call(functools.partial(kernel, rows, hi, lo, 16), out_shape=jax...]
where the time goes in v4:
time: 30.6 us; the launch traced here: 30.4 us
  Pallas kernels  28.8 us (94%)
  local copies, waits for them, and re-layouts  1.62 us (5%)
    pallas_call x1, Pallas kernels, body(): pl.pallas_call(functools.partial(kernel, rows, hi, lo, 16), out_shape=jax...  28.8 us
    unnamed x1, local copies, waits for them, and re-layouts  1.62 us

profile of v4, /device:TPU:1, one launch (start us, length us, event | category | flops | bytes accessed | tf_op | source)
XLA Modules:
  0.0 30.4 jit_solution(12257153903466355577)
XLA Ops:
  0.0 28.8 %shard_map.64 = f32[48,1024]{1,0:T(8,128)} custom-call(s32[4]{0:T(128)} %id1_ref.1, s32[4]{0:T(128)} %id2_ref.1, s32[4]{0:T(128)} %id3_ref.1, bf16[4,128,128,128]{3,2,1,0:T(8,128)(2,1)} %x_ref.1, bf16[48,1024]{1,0:T(8,128)(2,1)} %f2_ref.1, bf16[48,1024]{1,0:T(8,128)(2,1)} %f3_ref.1), custom_call_target="tpu_custom_call" | custom-call | tf_op jit(solution)/shard_map/pallas_call | solution.py:253
  28.8 1.6 %copy.8 = f32[48,1024]{1,0:T(8,128)} copy(f32[48,1024]{1,0:T(8,128)} %shard_map.64) | data formatting | bytes 393216

commit v5 on v4

--- a/solution.py
+++ b/solution.py
@@ -144,26 +144,68 @@
         owners.append(lax.div(block, jnp.int32(IB_DEV)))
         within.append(lax.rem(block[:1], jnp.int32(IB_DEV)))
 
+    row_id = lax.broadcasted_iota(jnp.int32, (rank, edge), 0)
+    lane_id = lax.broadcasted_iota(jnp.int32, (rank, edge), 1)
+
+    def gram_term(held, base, count):
+        part = jnp.concatenate([held[b] for b in range(base, min(base + 16, count))], axis=1)
+        return lax.dot_general(
+            part, part, (((1,), (1,)), ((), ())), preferred_element_type=jnp.float32
+        )
+
+    two_count, three_count = cols * two_blocks, rows * three_blocks
+    terms = [(0, f2g, base, two_count) for base in range(0, two_count, 16)]
+    terms += [(1, f3g, base, three_count) for base in range(0, three_count, 16)]
+
+    def first_work(grams):
+        system = grams[0] * grams[1]
+        work = jnp.concatenate([system, jnp.zeros((rank, edge - rank), jnp.float32)], axis=1)
+        work = work + jnp.where(lane_id == row_id, ridge_term, 0.0)
+        return work + jnp.where(lane_id == row_id + rank, 1.0, 0.0)
+
+    def eliminate(work, k):
+        first = jnp.broadcast_to(work[:, k : k + 1], (rank, edge))
+        second = jnp.broadcast_to(work[:, k + 1 : k + 2], (rank, edge))
+        row_a, row_b = work[k : k + 1], work[k + 1 : k + 2]
+        inv_a = 1.0 / first[k : k + 1]
+        cross = second[k : k + 1]
+        factor = first[k + 1 : k + 2] * inv_a
+        inv_b = 1.0 / (second[k + 1 : k + 2] - factor * cross)
+        new_b = (row_b - factor * row_a) * inv_b
+        new_a = (row_a - cross * new_b) * inv_a
+        work = work - first * new_a - second * new_b
+        return jnp.where(row_id == k, new_a, jnp.where(row_id == k + 1, new_b, work))
+
     slot_copies = []
     steps = half_edge // chunk
+    calls = steps * (tiles // 2)
+    grams = [jnp.zeros((rank, rank), jnp.float32)] * 2
+    work = None
     for part, (slots, landed) in enumerate(((slots_a, landed_a), (slots_b, landed_b))):
         packed = []
+        if part == 1:
+            work = first_work(grams)
         for pair in range(tiles // 2):
             if part == 0:
                 loads[2 * pair].wait()
                 loads[2 * pair + 1].wait()
 
-            def contract(step, _, pair=pair):
-                at = pl.ds(pl.multiple_of(step * chunk, chunk), chunk)
+            for step in range(steps):
+                at = pl.ds((part * steps + step) * chunk, chunk)
                 left = jnp.concatenate(
                     [xv[2 * pair + s, at].reshape(chunk * edge, edge) for s in range(2)], axis=1
                 )
                 contracted = jnp.dot(left, weights[pair], preferred_element_type=jnp.float32)
                 scaled = contracted.reshape(chunk, edge, edge) * scale[pair][None]
                 sums[pair, at, :] = jnp.sum(scaled, axis=1)
-                return 0
-
-            lax.fori_loop(part * steps, (part + 1) * steps, contract, 0, unroll=2)
+                call = pair * steps + step
+                if part == 0:
+                    for which, held, base, count in terms[call::calls]:
+                        grams[which] = grams[which] + gram_term(held, base, count)
+                else:
+                    pivots = rank // 2
+                    for k in range(pivots * call // calls, pivots * (call + 1) // calls):
+                        work = eliminate(work, 2 * k)
             turned = sums[pair, part * half_edge : (part + 1) * half_edge, :].T
             for s in range(2):
                 top = turned[s * rank : s * rank + half_rank]
@@ -188,37 +230,10 @@
                     )
                 )
 
-    def gram(held, count):
-        total = jnp.zeros((rank, rank), jnp.float32)
-        for base in range(0, count, 16):
-            part = jnp.concatenate([held[b] for b in range(base, min(base + 16, count))], axis=1)
-            total += lax.dot_general(
-                part, part, (((1,), (1,)), ((), ())), preferred_element_type=jnp.float32
-            )
-        return total
-
-    row_id = lax.broadcasted_iota(jnp.int32, (rank, edge), 0)
-    lane_id = lax.broadcasted_iota(jnp.int32, (rank, edge), 1)
-    system = gram(f2g, cols * two_blocks) * gram(f3g, rows * three_blocks)
-    padded = jnp.concatenate([system, jnp.zeros((rank, edge - rank), jnp.float32)], axis=1)
-    padded = padded + jnp.where(lane_id == row_id, ridge_term, 0.0)
-    work = padded + jnp.where(lane_id == row_id + rank, 1.0, 0.0)
-    for k in range(0, rank, 2):
-        first = jnp.broadcast_to(work[:, k : k + 1], (rank, edge))
-        second = jnp.broadcast_to(work[:, k + 1 : k + 2], (rank, edge))
-        row_a, row_b = work[k : k + 1], work[k + 1 : k + 2]
-        inv_a = 1.0 / first[k : k + 1]
-        cross = second[k : k + 1]
-        factor = first[k + 1 : k + 2] * inv_a
-        inv_b = 1.0 / (second[k + 1 : k + 2] - factor * cross)
-        new_b = (row_b - factor * row_a) * inv_b
-        new_a = (row_a - cross * new_b) * inv_a
-        work = work - first * new_a - second * new_b
-        work = jnp.where(row_id == k, new_a, jnp.where(row_id == k + 1, new_b, work))
     inverse = work[:, rank : 2 * rank]
-
     for copy in slot_copies:
         copy.wait_recv()
+    right = []
     for b in range(IB_DEV):
         first = jnp.zeros((half_rank, edge), jnp.float32)
         second = jnp.zeros((half_rank, edge), jnp.float32)
@@ -228,10 +243,11 @@
             second += jnp.where(hit, landed_b[i, :half_rank, :], 0.0)
         top = jnp.concatenate([first[:, :half_edge], second[:, :half_edge]], axis=1)
         low = jnp.concatenate([first[:, half_edge:], second[:, half_edge:]], axis=1)
-        out_ref[:, b * edge : (b + 1) * edge] = jnp.dot(
-            inverse, jnp.concatenate([top, low], axis=0),
-            preferred_element_type=jnp.float32, precision=lax.Precision.HIGHEST,
-        )
+        right.append(jnp.concatenate([top, low], axis=0))
+    out_ref[...] = jnp.dot(
+        inverse, jnp.concatenate(right, axis=1),
+        preferred_element_type=jnp.float32, precision=lax.Precision.HIGHEST,
+    )
     for copy in sent:
         copy.wait_send()
 

time: 30.6 us -> 30.3 us (level)
    pallas_call x1, Pallas kernels: 28.8 us -> 28.5 us  [body(): pl.pallas_call(functools.partial(kernel, rows, hi, lo, 16), out_shape=jax...]
where the time goes in v5:
time: 30.3 us; the launch traced here: 30.1 us
  Pallas kernels  28.5 us (94%)
  local copies, waits for them, and re-layouts  1.62 us (5%)
    pallas_call x1, Pallas kernels, body(): pl.pallas_call(functools.partial(kernel, rows, hi, lo, 16), out_shape=jax...  28.5 us
    unnamed x1, local copies, waits for them, and re-layouts  1.62 us

profile of v5, /device:TPU:1, one launch (start us, length us, event | category | flops | bytes accessed | tf_op | source)
XLA Modules:
  0.0 30.1 jit_solution(12819092354910140179)
XLA Ops:
  0.0 28.5 %shard_map.64 = f32[48,1024]{1,0:T(8,128)} custom-call(s32[4]{0:T(128)} %id1_ref.1, s32[4]{0:T(128)} %id2_ref.1, s32[4]{0:T(128)} %id3_ref.1, bf16[4,128,128,128]{3,2,1,0:T(8,128)(2,1)} %x_ref.1, bf16[48,1024]{1,0:T(8,128)(2,1)} %f2_ref.1, bf16[48,1024]{1,0:T(8,128)(2,1)} %f3_ref.1), custom_call_target="tpu_custom_call" | custom-call | tf_op jit(solution)/shard_map/pallas_call | solution.py:269
  28.5 1.6 %copy.8 = f32[48,1024]{1,0:T(8,128)} copy(f32[48,1024]{1,0:T(8,128)} %shard_map.64) | data formatting | bytes 393216
